TPU v7x, 32 devices: a whole 2x2x4 slice. The times are simulated.
32 devices in a mesh: leaf: 8 (over z, y), rhs: 4 (over x, core).
Axes of the slice: x: 2, y: 2, z: 4, core: 2. Of those that a mesh axis runs over, the one named last changes fastest.
Arguments:
- rhs_block: float32 [4096, 1024], P('leaf', 'rhs'), may hold values from -6 to 6
- leaf_order: int32 [8, 512], P('leaf'), may hold values from 0 to 511, as said below
- leaf_inverse: float32 [4096, 512], P('leaf'), may hold values from -0.04 to 3, as said below
- leaf_basis: float32 [4096, 128], P('leaf'), may hold values from -0.09678524 to 0.09678524
- transfer: bfloat16 [8, 2, 128, 128], P('leaf'), may hold values from -0.05 to 1.25, as said below
- precision: bfloat16 [8, 3, 128, 128], P('leaf'), may hold values from -0.09 to 8, as said below
Outputs:
- solution: float32 [4096, 1024], P('leaf', 'rhs')
Inputs may be any that keep to these rules, and one draw needn't show every extreme that they name: `leaf_order`: each row is a permutation of 0 to 511. `leaf_inverse`: each leaf's block of 512 x 512 entries is symmetric positive definite. transfer[b, k] is the same for all leaves b of one aligned group of 2 ** (k + 1) leaves. Every block is symmetric positive definite; precision[b, k] is the same for all leaves b of one aligned group of 2 ** (k + 1) leaves.
All inputs are finite; a program needn't handle non-finite values.
Results may differ from a plain program's by a relative error of at most 0.0003.
Values sent between devices are 32-bit elements; how exact they have to be, the bound alone decides.
No kernel may reach another device: no remote copies, remote signals or barrier semaphores. Data moves between devices by JAX's collectives and lax.ppermute only.
A program may use at most 64 MiB of HBM per device.

v0:
```python
import functools

import jax
import jax.numpy as jnp
from jax import lax
from jax.experimental import pallas as pl
from jax.experimental.pallas import tpu as pltpu
from jax.sharding import PartitionSpec as P

F32 = jnp.float32
BF16 = jnp.bfloat16
HIGH = lax.Precision.HIGH
SUB = 8
GIGA = 10 ** 9
VMEM = pl.BlockSpec(memory_space=pltpu.VMEM)
FAR = pl.BlockSpec(memory_space=pltpu.HBM)
PARAMS = pltpu.CompilerParams(vmem_limit_bytes=32 * 1024 * 1024)


def mm(a, b, precision=HIGH, dims=((1,), (0,))):
    return lax.dot_general(a, b, (dims, ((), ())), precision=precision, preferred_element_type=F32)


def split(x):
    top = x.astype(BF16)
    return top, (x - top.astype(F32)).astype(BF16)


def mm_parts(a, b):
    columns = b[0].shape[1]
    both = jnp.dot(a[0], jnp.concatenate(b, axis=1), preferred_element_type=F32)
    return both[:, :columns] + (both[:, columns:] + jnp.dot(a[1], b[0], preferred_element_type=F32))


def pick(mask, x):
    top, low = split(x)
    one = lambda part: lax.dot_general(mask, part, (((1,), (0,)), ((), ())), preferred_element_type=F32)
    return one(top) + one(low)


def reciprocal(x):
    return pltpu.reciprocal(x, approx=True)

def parts(x):
    top = x.astype(BF16).astype(F32)
    rest = x - top
    mid = rest.astype(BF16).astype(F32)
    return top, mid, rest - mid

def spread(x, k):
    return jnp.broadcast_to(x[:, k:k + 1], x.shape)


def four(x, y, cols, at, k, lane, row, hold):
    size = x.shape[1]
    across = size // SUB * SUB
    inside = (lane >= k) & (lane < k + 4)
    own = (row >= at) & (row < at + 4)
    ahead = [(k + 4 + j) % across for j in range(4)]
    coming = [spread(x, a) for a in ahead]
    down = [spread(y, k + j) for j in range(4)]
    hold[8] = x
    for j in range(4):
        hold[j] = cols[j]
        hold[4 + j] = coming[j]
    line = lambda j, i: jnp.broadcast_to(hold[j, at + i:at + i + 1], (SUB, size))
    a0, a1, a2 = line(0, 0), line(1, 0), line(1, 1)
    b00, b01, b10, b11 = line(0, 2), line(1, 2), line(0, 3), line(1, 3)
    c0, c1, c2 = line(2, 2), line(3, 2), line(3, 3)
    det = a0 * a2 - a1 * a1
    g00, g01 = b00 * a2 - b01 * a1, b01 * a0 - b00 * a1
    g10, g11 = b10 * a2 - b11 * a1, b11 * a0 - b10 * a1
    s0 = det * c0 - (g00 * b00 + g01 * b01)
    s1 = det * c1 - (g00 * b10 + g01 * b11)
    s2 = det * c2 - (g10 * b10 + g11 * b11)
    rs = reciprocal(s0 * s2 - s1 * s1)
    ra = reciprocal(det)

    def solve(e):
        t2 = det * e[2] - (g00 * e[0] + g01 * e[1])
        t3 = det * e[3] - (g10 * e[0] + g11 * e[1])
        w2 = (s2 * t2 - s1 * t3) * rs
        w3 = (s0 * t3 - s1 * t2) * rs
        w0 = ((a2 * e[0] - a1 * e[1]) - (g00 * w2 + g10 * w3)) * ra
        w1 = ((a0 * e[1] - a1 * e[0]) - (g01 * w2 + g11 * w3)) * ra
        return w0, w1, w2, w3

    less = lambda base, c, w: (base - (c[2] * w[2] + c[3] * w[3])) - (c[0] * w[0] + c[1] * w[1])
    cols = [jnp.where(own, jnp.where(row == at + j, -1.0, 0.0), cols[j]) for j in range(4)]
    there = [solve([line(4 + j, i) for i in range(4)]) for j in range(4)]
    if at + 4 < SUB:
        after = [less(jnp.where(own, 0.0, coming[j]), cols, there[j]) for j in range(4)]
    else:
        after = [less(spread(y, ahead[j]), down, there[j]) for j in range(4)]
    w = solve([jnp.where(inside, jnp.where(lane == k + j, 1.0, 0.0), line(8, j)) for j in range(4)])
    x = less(jnp.where(inside | own, 0.0, x), cols, w)
    y = less(jnp.where(inside, 0.0, y), down, w)
    return x, y, after


def invert(m, xt, w6, wide_w, hold):
    size = m.shape[0]
    lane = lax.broadcasted_iota(jnp.int32, (SUB, size), 1)
    row = lax.broadcasted_iota(jnp.int32, (SUB, size), 0)
    wide = lax.broadcasted_iota(jnp.int32, (size, size), 1)
    count = size // SUB

    def trail(t):
        k = t * SUB
        u = jnp.dot(xt[...], w6[...], preferred_element_type=F32)
        m[...] = jnp.where((wide >= k) & (wide < k + SUB), 0.0, m[...]) - u

    def step(t, carry):
        x, *cols = carry
        k = t * SUB
        before = k - SUB
        y = m[pl.ds((t + 1) % count * SUB, SUB)]
        terms = [spread(y, max(before, 0) + j) * jnp.broadcast_to(wide_w[j:j + 1], (SUB, size)) for j in range(SUB)]
        y = jnp.where((lane >= before) & (lane < k), 0.0, y)
        y = y - (((terms[0] + terms[1]) + (terms[2] + terms[3])) + ((terms[4] + terms[5]) + (terms[6] + terms[7])))
        trail(t - 1)
        z = jnp.where(lane < k, -1.0, 1.0) * x
        z = jnp.where((lane >= k) & (lane < k + SUB), jnp.where(lane - k == row, -1.0, 0.0), z)
        h, n, l = parts(z)
        xt[...] = jnp.concatenate([h, h, n, n, h, l], axis=0).astype(BF16).T
        for g in range(0, SUB, 4):
            x, y, cols = four(x, y, cols, g, k + g, lane, row, hold.at[g // 4])
        h, n, l = parts(x)
        w6[...] = jnp.concatenate([h, n, h, n, l, h], axis=0).astype(BF16)
        wide_w[...] = x
        m[pl.ds(k, SUB)] = jnp.zeros((SUB, size), F32)
        return y, *cols

    xt[...] = jnp.zeros(xt.shape, BF16)
    w6[...] = jnp.zeros(w6.shape, BF16)
    wide_w[...] = jnp.zeros((SUB, size), F32)
    x = m[0:SUB]
    carry = (x, *(spread(x, j) for j in range(4)))
    for t in range(count):
        carry = step(t, carry)
    trail(count - 1)


def invert_scratch(size):
    return [
        pltpu.VMEM((size, size), F32), pltpu.VMEM((size, 6 * SUB), BF16), pltpu.VMEM((6 * SUB, size), BF16),
        pltpu.VMEM((SUB, size), F32), pltpu.VMEM((SUB // 4, 9, SUB, size), F32),
    ]


def scaled_inverse(matrix, *work):
    size = matrix.shape[0]
    rows = lax.broadcasted_iota(jnp.int32, (size, size), 0)
    cols = lax.broadcasted_iota(jnp.int32, (size, size), 1)
    diagonal = jnp.where(rows == cols, matrix, 0.0)
    down = lax.rsqrt(jnp.sum(diagonal, axis=1, keepdims=True))
    across = lax.rsqrt(jnp.sum(diagonal, axis=0, keepdims=True))
    work[0][...] = matrix * down * across
    invert(*work)
    return work[0][...] * down * across


def basis_kernel(pieces, inverse_far, basis_far, order_far, top, low, basis_t, order, carried, gram, inverse, basis, sems):
    rows = inverse.shape[0] // pieces
    copies = [pltpu.make_async_copy(basis_far, basis, sems.at[pieces])]
    for i in range(pieces):
        part = pl.ds(i * rows, rows)
        copies.append(pltpu.make_async_copy(inverse_far.at[part], inverse.at[part], sems.at[i]))
    copies.append(pltpu.make_async_copy(order_far, order, sems.at[pieces + 1]))
    for copy in copies:
        copy.start()
    copies[0].wait()
    basis_parts = split(basis[...])
    across = basis[...].T
    basis_t[...] = across
    across = split(across)
    for i in range(pieces):
        part = slice(i * rows, (i + 1) * rows)
        copies[i + 1].wait()
        block = split(inverse[part])
        top[part], low[part] = block
        carried[part] = mm_parts(block, basis_parts)
    gram[...] = mm_parts(across, split(carried[...]))
    copies[-1].wait()


def leaf_kernel(order, rhs, top, low, basis_t, solved, projected):
    points = rhs.shape[0]
    wide = 128
    numbers = order[...].astype(F32)
    lanes = lax.broadcasted_iota(jnp.int32, (wide, points), 1).astype(F32)
    gather = []
    for i in range(0, points, wide):
        column = jnp.broadcast_to(numbers[:, i:i + wide], (wide, wide)).T
        column = jnp.concatenate([column] * (points // wide), axis=1)
        gather.append(jnp.where(column == lanes, 1.0, 0.0).astype(BF16))
    ordered = pick(jnp.concatenate(gather, axis=0), rhs[...])
    z = mm_parts((top[...], low[...]), split(ordered))
    solved[...] = z
    projected[...] = mm(basis_t[...], z)


def place_kernel(order, solved, carried, solved_out, carried_out):
    points = solved.shape[0]
    rows = lax.broadcasted_iota(jnp.int32, (points, points), 0)
    scatter = jnp.where(order[...] == rows, 1.0, 0.0).astype(BF16)
    solved_out[...] = pick(scatter, solved[...])
    carried_out[...] = pick(scatter, carried[...])


def node_kernel(level, gram, other, precision, *rest):
    coupling = precision[0, level].astype(F32)
    whole = gram[...] + other[...]
    if len(rest) == 6:
        rest[0][...] = scaled_inverse(coupling + whole, *rest[1:])
        return
    transfer, inverse, mover, gram_out, *work = rest
    mixer = transfer[0, level]
    left = mm(mixer, precision[0, level], None, ((0,), (0,)))
    right = sum(mm(part.astype(BF16), mixer, None) for part in parts(whole))
    m = scaled_inverse(coupling + whole, *work)
    n = mm(left, m)
    inverse[...] = m
    mover[...] = n
    gram_out[...] = mm(n, right)


def lift_kernel(first, last, *refs):
    refs = list(refs)
    projected, other, inverse, mover = (ref[...] for ref in refs[:4])
    s = projected + other
    alpha = mm(inverse, s)
    projected_out, total_out, mixing_out = refs[-3:]
    projected_out[...] = mm(mover, s)
    if first:
        total, mixing = alpha, mover.T
    else:
        total, mixing = refs[4][...], refs[5][...]
        total = total + mm(mixing, alpha)
        mixing = mm(mixing, mover, HIGH, ((1,), (1,)))
    if last:
        solved, carried = refs[-5:-3]
        total = solved[...] - mm(carried[...], total)
        mixing = mm(carried[...], mixing)
    total_out[...] = total
    mixing_out[...] = mixing


def root_kernel(pieces, projected, other, inverse, solved, carried, out_far, out, sems):
    alpha = mm(inverse[...], projected[...] + other[...])
    rows = out.shape[0] // pieces
    copies = []
    for i in range(pieces):
        part = pl.ds(i * rows, rows)
        out[part] = solved[part] - mm(carried[part], alpha)
        copies.append(pltpu.make_async_copy(out.at[part], out_far.at[part], sems.at[i]))
        copies[-1].start()
    for copy in copies:
        copy.wait()


def call(kernel, outs, *args, scratch=(), work=0, place=VMEM, result=VMEM, after=()):
    if place is FAR:
        args = [pltpu.with_memory_space_constraint(arg, pltpu.HBM) for arg in args]
    return pl.pallas_call(
        lambda *refs: kernel(*refs[len(after):]),
        out_shape=[jax.ShapeDtypeStruct(getattr(out, "shape", out), getattr(out, "dtype", F32)) for out in outs],
        in_specs=[FAR] * len(after) + [place] * len(args),
        out_specs=[result] * len(outs),
        scratch_shapes=scratch,
        cost_estimate=pl.CostEstimate(flops=work, bytes_accessed=0, transcendentals=0),
        compiler_params=PARAMS,
    )(*after, *args)


def from_partner(block, axis, apart):
    count = lax.axis_size(axis)
    return lax.ppermute(block, axis, [(i, i ^ 1 << apart) for i in range(count)])


def body(rhs, order, inverse, basis, transfer, precision):
    points, columns = rhs.shape
    rank = basis.shape[1]
    square, tall, block = (rank, rank), (points, rank), (rank, columns)
    levels = lax.axis_size("leaf").bit_length() - 1
    pieces = 2
    half = jax.ShapeDtypeStruct(inverse.shape, BF16)
    top, low, basis_t, order, carried, gram = call(
        functools.partial(basis_kernel, pieces), [half, half, (rank, points), order, tall, square],
        inverse, basis, order, place=FAR, work=GIGA,
        scratch=[pltpu.VMEM(inverse.shape, F32), pltpu.VMEM(tall, F32), pltpu.SemaphoreType.DMA((pieces + 2,))]
    )
    other_gram = from_partner(gram, "leaf", 0)
    solved, projected = call(leaf_kernel, [rhs, block], order, rhs, top, low, basis_t, work=2 * GIGA)
    place = lambda *after: call(place_kernel, [rhs, tall], order, solved, carried, work=GIGA, after=after)
    if levels < 3:
        solved, carried = place()
    state, after = (), ()
    for k in range(levels - 1):
        other = from_partner(projected, "leaf", k)
        m, n, gram = call(
            functools.partial(node_kernel, k), [square] * 3, gram, other_gram, precision, transfer,
            scratch=invert_scratch(rank), work=6 * GIGA, after=after
        )
        other_gram = from_partner(gram, "leaf", k + 1)
        last = k == levels - 2
        projected, *state = call(
            functools.partial(lift_kernel, k == 0, last),
            [block, (points, columns), tall] if last else [block, block, square],
            projected, other, m, n, *state, *((solved, carried) if last else ()), work=GIGA
        )
        if k == 0 and not last:
            solved, carried = place(projected)
            after = (carried,)
    solved, carried = state or (solved, carried)
    k = levels - 1
    other = from_partner(projected, "leaf", k)
    (m,) = call(functools.partial(node_kernel, k), [square], gram, other_gram, precision, scratch=invert_scratch(rank), work=6 * GIGA)
    (out,) = call(
        functools.partial(root_kernel, pieces), [rhs], projected, other, m, solved, carried, work=GIGA, result=FAR,
        scratch=[pltpu.VMEM(rhs.shape, F32), pltpu.SemaphoreType.DMA((pieces,))]
    )
    return out


def solution(mesh):
    placed = (
        P("leaf", "rhs"),
        P("leaf", None),
        P("leaf", None),
        P("leaf", None),
        P("leaf", None, None, None),
        P("leaf", None, None, None),
    )
    return jax.shard_map(
        body, mesh=mesh, in_specs=placed, out_specs=P("leaf", "rhs"), check_vma=False
    )
```

profile of v0, /device:TPU:0, one launch (start us, length us, event | category | flops | bytes accessed | tf_op | source)
XLA Modules:
  0.0 34.4 jit_solution(13762688822916655666)
XLA Ops:
  0.0 2.0 %shard_map.64 = (bf16[512,512]{1,0:T(8,128)(2,1)S(1)}, bf16[512,512]{1,0:T(8,128)(2,1)S(1)}, f32[128,512]{1,0:T(8,128)S(1)}, s32[1,512]{1,0:T(1,128)S(1)}, f32[5...) custom-call(f32[512,512]{1,0:T(8,128)} %refs_0_.1, f32[512,128]{1,0:T(8,128)} %refs_1_.2, s32[1,512]{1,0:T(1,128)} %refs_2_.3), custom_call_target="tpu_custom_call" | custom-call | flops 1000000000 | tf_op jit(solution)/shard_map/pallas_call | solution.py:265
  2.0 3.0 %collective-permute-start.1 = (f32[128,128]{1,0:T(8,128)S(1)}, f32[128,128]{1,0:T(8,128)S(1)}, u32[]{:S(2)}, u32[]{:S(2)}) collective-permute-start(f32[128,128]{1,0:T(8,128)S(1)} %get-tuple-element.32.refs_0_), channel_id=1, source_target_pairs={{0,4},{4,0},{8,12},{12,8},{16,20},{20,16},{24,28},{28,24},{1,5},{5... | collective-permute-start | bytes 196616 | tf_op jit(solution)/shard_map/ppermute | solution.py:278
  5.0 0.0 copy-done
  5.0 1.8 %shard_map.65 = (f32[512,256]{1,0:T(8,128)S(1)}, f32[128,256]{1,0:T(8,128)S(1)}) custom-call(s32[1,512]{1,0:T(1,128)S(1)} %get-tuple-element.27.refs_0_.refs_1_, f32[512,256]{1,0:T(8,128)S(1)} %copy-done, bf16[512,512]{1,0:T(8,128)(2,1)S(1)} %get-tuple-element.28.refs_2_, bf16[512,512]{1,0:T(8,128)(2,1)S(1)} %get-tuple-element.29.refs_3_, ...), custom_call_target="tpu_custom_call" | custom-call | flops 2000000000 | tf_op jit(solution)/shard_map/pallas_call | solution.py:265
  6.9 0.1 collective-permute-start
  7.0 0.3 collective-permute-done.1.refs_1_
  7.3 0.0 copy-done.1
  7.3 0.0 copy-done.2
  7.3 4.3 %shard_map.66 = (f32[128,128]{1,0:T(8,128)S(1)}, f32[128,128]{1,0:T(8,128)S(1)}, f32[128,128]{1,0:T(8,128)S(1)}) custom-call(f32[128,128]{1,0:T(8,128)S(1)} %get-tuple-element.32.refs_0_, f32[128,128]{1,0:T(8,128)S(1)} %collective-permute-done.1.refs_1_, bf16[1,3,128,128]{3,2,1,0:T(8,128)(2,1)S(1)} %copy-done.1, bf16[1,2,128,128]{3,2,1,0:T(8,128)(2,1)S(1)} %copy-done.2), custom_call_target="tpu_custom_call" | custom-call | flops 6000000000 | tf_op jit(solution)/shard_map/pallas_call | solution.py:265
  11.6 2.1 %collective-permute-start.3 = (f32[128,128]{1,0:T(8,128)S(1)}, f32[128,128]{1,0:T(8,128)S(1)}, u32[]{:S(2)}, u32[]{:S(2)}) collective-permute-start(f32[128,128]{1,0:T(8,128)S(1)} %get-tuple-element.39.refs_1_), channel_id=1, source_target_pairs={{0,8},{4,12},{8,0},{12,4},{16,24},{20,28},{24,16},{28,20},{1,9},{5... | collective-permute-start | bytes 196616 | tf_op jit(solution)/shard_map/ppermute | solution.py:278
  13.7 0.0 collective-permute-done.refs_1_
  13.7 0.3 shard_map.67
  14.0 0.1 collective-permute-start.2
  14.1 0.7 %shard_map.68 = (f32[512,256]{1,0:T(8,128)S(1)}, f32[512,128]{1,0:T(8,128)S(1)}) custom-call(f32[128,256]{1,0:T(8,128)S(1)} %get-tuple-element.35.refs_0_, s32[1,512]{1,0:T(1,128)S(1)} %get-tuple-element.27.refs_0_.refs_1_, f32[512,256]{1,0:T(8,128)S(1)} %get-tuple-element.36.refs_2_, f32[512,128]{1,0:T(8,128)S(1)} %get-tuple-element.37.refs_3_), custom_call_target="tpu_custom_call" | custom-call | flops 1000000000 | tf_op jit(solution)/shard_map/pallas_call | solution.py:265
  14.8 1.8 %collective-permute-done.3.refs_2_ = f32[128,128]{1,0:T(8,128)S(1)} collective-permute-done((f32[128,128]{1,0:T(8,128)S(1)}, f32[128,128]{1,0:T(8,128)S(1)}, u32[]{:S(2)}, u32[]{:S(2)}) %collective-permute-start.3) | collective-permute-done | bytes 65568 | tf_op jit(solution)/shard_map/ppermute | solution.py:278
  16.6 4.3 %shard_map.69 = (f32[128,128]{1,0:T(8,128)S(1)}, f32[128,128]{1,0:T(8,128)S(1)}, f32[128,128]{1,0:T(8,128)S(1)}) custom-call(f32[512,128]{1,0:T(8,128)S(1)} %get-tuple-element.38.refs_0_.refs_7_, f32[128,128]{1,0:T(8,128)S(1)} %get-tuple-element.39.refs_1_, f32[128,128]{1,0:T(8,128)S(1)} %collective-permute-done.3.refs_2_, ...), custom_call_target="tpu_custom_call" | custom-call | flops 6000000000 | tf_op jit(solution)/shard_map/pallas_call | solution.py:265
  20.9 3.1 %collective-permute-start.5 = (f32[128,128]{1,0:T(8,128)S(1)}, f32[128,128]{1,0:T(8,128)S(1)}, u32[]{:S(2)}, u32[]{:S(2)}) collective-permute-start(f32[128,128]{1,0:T(8,128)S(1)} %get-tuple-element.46.refs_0_), channel_id=1, source_target_pairs={{0,16},{4,20},{8,24},{12,28},{16,0},{20,4},{24,8},{28,12},{1,17},{... | collective-permute-start | bytes 196616 | tf_op jit(solution)/shard_map/ppermute | solution.py:278
  24.0 0.0 collective-permute-done.2.refs_1_
  24.0 0.9 %shard_map.70 = (f32[128,256]{1,0:T(8,128)S(1)}, f32[512,256]{1,0:T(8,128)S(1)}, f32[512,128]{1,0:T(8,128)S(1)}) custom-call(f32[128,256]{1,0:T(8,128)S(1)} %get-tuple-element.35.refs_0_, f32[128,256]{1,0:T(8,128)S(1)} %collective-permute-done.2.refs_1_, f32[128,128]{1,0:T(8,128)S(1)} %get-tuple-element.40.refs_2_, ...), custom_call_target="tpu_custom_call" | custom-call | flops 1000000000 | tf_op jit(solution)/shard_map/pallas_call | solution.py:265
  24.9 0.1 collective-permute-start.4
  25.0 4.0 %collective-permute-done.5.refs_1_ = f32[128,128]{1,0:T(8,128)S(1)} collective-permute-done((f32[128,128]{1,0:T(8,128)S(1)}, f32[128,128]{1,0:T(8,128)S(1)}, u32[]{:S(2)}, u32[]{:S(2)}) %collective-permute-start.5) | collective-permute-done | bytes 65568 | tf_op jit(solution)/shard_map/ppermute | solution.py:278
  29.0 4.0 %shard_map.71.refs_2_ = f32[128,128]{1,0:T(8,128)S(1)} custom-call(f32[128,128]{1,0:T(8,128)S(1)} %get-tuple-element.46.refs_0_, f32[128,128]{1,0:T(8,128)S(1)} %collective-permute-done.5.refs_1_, bf16[1,3,128,128]{3,2,1,0:T(8,128)(2,1)S(1)} %copy-done.1), custom_call_target="tpu_custom_call" | custom-call | flops 6000000000 | tf_op jit(solution)/shard_map/pallas_call | solution.py:265
  33.0 0.0 collective-permute-done.4.refs_1_
  33.0 1.4 %shard_map.72 = f32[512,256]{1,0:T(8,128)} custom-call(f32[128,256]{1,0:T(8,128)S(1)} %get-tuple-element.45.refs_0_, f32[128,256]{1,0:T(8,128)S(1)} %collective-permute-done.4.refs_1_, f32[128,128]{1,0:T(8,128)S(1)} %shard_map.71.refs_2_, f32[512,256]{1,0:T(8,128)S(1)} %get-tuple-element.47.refs_3_, f32[512,128]{1,0:T(8,128)S(1)} %get-tuple-element.48.refs_4_), custom_call_target="tpu_custom_call" | custom-call | flops 1000000000 | tf_op jit(solution)/shard_map/pallas_call | solution.py:265
  (3 shorter events, 0.0 us)
Async XLA Ops:
  0.0 5.0 %copy-start = (f32[512,256]{1,0:T(8,128)S(1)}, f32[512,256]{1,0:T(8,128)}, u32[]{:S(2)}) copy-start(f32[512,256]{1,0:T(8,128)} %refs_1_.3) | copy-start | bytes 1572868
  2.0 5.3 %collective-permute-start.1 = (f32[128,128]{1,0:T(8,128)S(1)}, f32[128,128]{1,0:T(8,128)S(1)}, u32[]{:S(2)}, u32[]{:S(2)}) collective-permute-start(f32[128,128]{1,0:T(8,128)S(1)} %get-tuple-element.32.refs_0_), channel_id=1, source_target_pairs={{0,4},{4,0},{8,12},{12,8},{16,20},{20,16},{24,28},{28,24},{1,5},{5... | collective-permute-start | bytes 196616 | tf_op jit(solution)/shard_map/ppermute | solution.py:278
  5.0 2.2 %copy-start.1 = (bf16[1,3,128,128]{3,2,1,0:T(8,128)(2,1)S(1)}, bf16[1,3,128,128]{3,2,1,0:T(8,128)(2,1)}, u32[]{:S(2)}) copy-start(bf16[1,3,128,128]{3,2,1,0:T(8,128)(2,1)} %refs_2_.5) | copy-start | bytes 294916
  5.0 2.2 %copy-start.2 = (bf16[1,2,128,128]{3,2,1,0:T(8,128)(2,1)S(1)}, bf16[1,2,128,128]{3,2,1,0:T(8,128)(2,1)}, u32[]{:S(2)}) copy-start(bf16[1,2,128,128]{3,2,1,0:T(8,128)(2,1)} %refs_4_.1) | copy-start | bytes 196612
  6.9 6.9 %collective-permute-start = (f32[128,256]{1,0:T(8,128)S(1)}, f32[128,256]{1,0:T(8,128)S(1)}, u32[]{:S(2)}, u32[]{:S(2)}) collective-permute-start(f32[128,256]{1,0:T(8,128)S(1)} %get-tuple-element.31.refs_0_), channel_id=1, source_target_pairs={{0,4},{4,0},{8,12},{12,8},{16,20},{20,16},{24,28},{28,24},{1,5},{5... | collective-permute-start | bytes 393224 | tf_op jit(solution)/shard_map/ppermute | solution.py:278
  11.6 5.0 %collective-permute-start.3 = (f32[128,128]{1,0:T(8,128)S(1)}, f32[128,128]{1,0:T(8,128)S(1)}, u32[]{:S(2)}, u32[]{:S(2)}) collective-permute-start(f32[128,128]{1,0:T(8,128)S(1)} %get-tuple-element.39.refs_1_), channel_id=1, source_target_pairs={{0,8},{4,12},{8,0},{12,4},{16,24},{20,28},{24,16},{28,20},{1,9},{5... | collective-permute-start | bytes 196616 | tf_op jit(solution)/shard_map/ppermute | solution.py:278
  14.0 10.0 %collective-permute-start.2 = (f32[128,256]{1,0:T(8,128)S(1)}, f32[128,256]{1,0:T(8,128)S(1)}, u32[]{:S(2)}, u32[]{:S(2)}) collective-permute-start(f32[128,256]{1,0:T(8,128)S(1)} %get-tuple-element.35.refs_0_), channel_id=1, source_target_pairs={{0,8},{4,12},{8,0},{12,4},{16,24},{20,28},{24,16},{28,20},{1,9},{5... | collective-permute-start | bytes 393224 | tf_op jit(solution)/shard_map/ppermute | solution.py:278
  20.9 8.1 %collective-permute-start.5 = (f32[128,128]{1,0:T(8,128)S(1)}, f32[128,128]{1,0:T(8,128)S(1)}, u32[]{:S(2)}, u32[]{:S(2)}) collective-permute-start(f32[128,128]{1,0:T(8,128)S(1)} %get-tuple-element.46.refs_0_), channel_id=1, source_target_pairs={{0,16},{4,20},{8,24},{12,28},{16,0},{20,4},{24,8},{28,12},{1,17},{... | collective-permute-start | bytes 196616 | tf_op jit(solution)/shard_map/ppermute | solution.py:278
  24.9 8.1 %collective-permute-start.4 = (f32[128,256]{1,0:T(8,128)S(1)}, f32[128,256]{1,0:T(8,128)S(1)}, u32[]{:S(2)}, u32[]{:S(2)}) collective-permute-start(f32[128,256]{1,0:T(8,128)S(1)} %get-tuple-element.45.refs_0_), channel_id=1, source_target_pairs={{0,16},{4,20},{8,24},{12,28},{16,0},{20,4},{24,8},{28,12},{1,17},{... | collective-permute-start | bytes 393224 | tf_op jit(solution)/shard_map/ppermute | solution.py:278
where the time goes:
time: 34.5 us; the launch traced here: 34.4 us
  Pallas kernels  19.6 us (57%)
  starting transfers between devices  8.51 us (25%)
  waiting for transfers between devices  6.19 us (18%)
    pallas_call x9, Pallas kernels, call(): pl.pallas_call(lambda *refs: kernel(*refs[len(after):]), out_shape=[jax.S...  19.6 us
    ppermute x6, starting transfers between devices, from_partner(): lax.ppermute(block, axis, [(i, i ^ 1 << apart) for i in range(count)])  8.51 us
    ppermute x6, waiting for transfers between devices, from_partner(): lax.ppermute(block, axis, [(i, i ^ 1 << apart) for i in range(count)])  6.19 us
  transfers between devices with their start and end apart: 6, of which 3 were waited for; matrix products, arithmetic and copies ran while one was open for 0% of the time, Pallas kernels for 47%

commit v1 on v0

--- a/solution.py
+++ b/solution.py
@@ -76,25 +76,27 @@
     rs = reciprocal(s0 * s2 - s1 * s1)
     ra = reciprocal(det)
 
-    def solve(e):
+    def known(e):
         t2 = det * e[2] - (g00 * e[0] + g01 * e[1])
         t3 = det * e[3] - (g10 * e[0] + g11 * e[1])
-        w2 = (s2 * t2 - s1 * t3) * rs
-        w3 = (s0 * t3 - s1 * t2) * rs
-        w0 = ((a2 * e[0] - a1 * e[1]) - (g00 * w2 + g10 * w3)) * ra
-        w1 = ((a0 * e[1] - a1 * e[0]) - (g01 * w2 + g11 * w3)) * ra
-        return w0, w1, w2, w3
-
-    less = lambda base, c, w: (base - (c[2] * w[2] + c[3] * w[3])) - (c[0] * w[0] + c[1] * w[1])
-    cols = [jnp.where(own, jnp.where(row == at + j, -1.0, 0.0), cols[j]) for j in range(4)]
-    there = [solve([line(4 + j, i) for i in range(4)]) for j in range(4)]
+        return a2 * e[0] - a1 * e[1], a0 * e[1] - a1 * e[0], s2 * t2 - s1 * t3, s0 * t3 - s1 * t2
+
+    def second(c):
+        return c[0], c[1], c[2] - (c[0] * g00 + c[1] * g01) * ra, c[3] - (c[0] * g10 + c[1] * g11) * ra
+
+    def less(base, c, v):
+        return (base - (c[0] * v[0] + c[1] * v[1]) * ra) - (c[2] * v[2] + c[3] * v[3]) * rs
+
+    cols = second([jnp.where(own, jnp.where(row == at + j, -1.0, 0.0), cols[j]) for j in range(4)])
+    down = second(down)
+    there = [known([line(4 + j, i) for i in range(4)]) for j in range(4)]
     if at + 4 < SUB:
         after = [less(jnp.where(own, 0.0, coming[j]), cols, there[j]) for j in range(4)]
     else:
         after = [less(spread(y, ahead[j]), down, there[j]) for j in range(4)]
-    w = solve([jnp.where(inside, jnp.where(lane == k + j, 1.0, 0.0), line(8, j)) for j in range(4)])
-    x = less(jnp.where(inside | own, 0.0, x), cols, w)
-    y = less(jnp.where(inside, 0.0, y), down, w)
+    here = known([jnp.where(inside, jnp.where(lane == k + j, 1.0, 0.0), line(8, j)) for j in range(4)])
+    x = less(jnp.where(inside | own, 0.0, x), cols, here)
+    y = less(jnp.where(inside, 0.0, y), down, here)
     return x, y, after
 
 

time: 34.5 us -> 34.1 us (0.988)
  Pallas kernels: 19.6 us -> 19.2 us
    pallas_call x9, Pallas kernels: 19.6 us -> 19.2 us  [call(): pl.pallas_call(lambda *refs: kernel(*refs[len(after):]), out_shape=[jax.S...]
  transfers between devices with their start and end apart: 6 -> 6, of which waited for: 3 -> 3; matrix products, arithmetic and copies ran while one was open for 0% -> 0% of each run, Pallas kernels for 47% -> 46%
where the time goes in v1:
time: 34.1 us; the launch traced here: 34 us
  Pallas kernels  19.2 us (56%)
  starting transfers between devices  8.52 us (25%)
  waiting for transfers between devices  6.19 us (18%)
    pallas_call x9, Pallas kernels, call(): pl.pallas_call(lambda *refs: kernel(*refs[len(after):]), out_shape=[jax.S...  19.2 us
    ppermute x6, starting transfers between devices, from_partner(): lax.ppermute(block, axis, [(i, i ^ 1 << apart) for i in range(count)])  8.52 us
    ppermute x6, waiting for transfers between devices, from_partner(): lax.ppermute(block, axis, [(i, i ^ 1 << apart) for i in range(count)])  6.19 us
  transfers between devices with their start and end apart: 6, of which 3 were waited for; matrix products, arithmetic and copies ran while one was open for 0% of the time, Pallas kernels for 46%

profile of v1, /device:TPU:0, one launch (start us, length us, event | category | flops | bytes accessed | tf_op | source)
XLA Modules:
  0.0 34.0 jit_solution(11519075237659851207)
XLA Ops:
  0.0 2.0 %shard_map.64 = (bf16[512,512]{1,0:T(8,128)(2,1)S(1)}, bf16[512,512]{1,0:T(8,128)(2,1)S(1)}, f32[128,512]{1,0:T(8,128)S(1)}, s32[1,512]{1,0:T(1,128)S(1)}, f32[5...) custom-call(f32[512,512]{1,0:T(8,128)} %refs_0_.1, f32[512,128]{1,0:T(8,128)} %refs_1_.2, s32[1,512]{1,0:T(1,128)} %refs_2_.3), custom_call_target="tpu_custom_call" | custom-call | flops 1000000000 | tf_op jit(solution)/shard_map/pallas_call | solution.py:267
  2.0 3.0 %collective-permute-start.1 = (f32[128,128]{1,0:T(8,128)S(1)}, f32[128,128]{1,0:T(8,128)S(1)}, u32[]{:S(2)}, u32[]{:S(2)}) collective-permute-start(f32[128,128]{1,0:T(8,128)S(1)} %get-tuple-element.32.refs_0_), channel_id=1, source_target_pairs={{0,4},{4,0},{8,12},{12,8},{16,20},{20,16},{24,28},{28,24},{1,5},{5... | collective-permute-start | bytes 196616 | tf_op jit(solution)/shard_map/ppermute | solution.py:280
  5.0 0.0 copy-done
  5.0 1.8 %shard_map.65 = (f32[512,256]{1,0:T(8,128)S(1)}, f32[128,256]{1,0:T(8,128)S(1)}) custom-call(s32[1,512]{1,0:T(1,128)S(1)} %get-tuple-element.27.refs_0_.refs_1_, f32[512,256]{1,0:T(8,128)S(1)} %copy-done, bf16[512,512]{1,0:T(8,128)(2,1)S(1)} %get-tuple-element.28.refs_2_, bf16[512,512]{1,0:T(8,128)(2,1)S(1)} %get-tuple-element.29.refs_3_, ...), custom_call_target="tpu_custom_call" | custom-call | flops 2000000000 | tf_op jit(solution)/shard_map/pallas_call | solution.py:267
  6.9 0.1 collective-permute-start
  7.0 0.3 collective-permute-done.1.refs_1_
  7.3 0.0 copy-done.1
  7.3 0.0 copy-done.2
  7.3 4.1 %shard_map.66 = (f32[128,128]{1,0:T(8,128)S(1)}, f32[128,128]{1,0:T(8,128)S(1)}, f32[128,128]{1,0:T(8,128)S(1)}) custom-call(f32[128,128]{1,0:T(8,128)S(1)} %get-tuple-element.32.refs_0_, f32[128,128]{1,0:T(8,128)S(1)} %collective-permute-done.1.refs_1_, bf16[1,3,128,128]{3,2,1,0:T(8,128)(2,1)S(1)} %copy-done.1, bf16[1,2,128,128]{3,2,1,0:T(8,128)(2,1)S(1)} %copy-done.2), custom_call_target="tpu_custom_call" | custom-call | flops 6000000000 | tf_op jit(solution)/shard_map/pallas_call | solution.py:267
  11.4 2.1 %collective-permute-start.3 = (f32[128,128]{1,0:T(8,128)S(1)}, f32[128,128]{1,0:T(8,128)S(1)}, u32[]{:S(2)}, u32[]{:S(2)}) collective-permute-start(f32[128,128]{1,0:T(8,128)S(1)} %get-tuple-element.39.refs_1_), channel_id=1, source_target_pairs={{0,8},{4,12},{8,0},{12,4},{16,24},{20,28},{24,16},{28,20},{1,9},{5... | collective-permute-start | bytes 196616 | tf_op jit(solution)/shard_map/ppermute | solution.py:280
  13.6 0.0 collective-permute-done.refs_1_
  13.6 0.3 shard_map.67
  13.8 0.1 collective-permute-start.2
  13.9 0.7 %shard_map.68 = (f32[512,256]{1,0:T(8,128)S(1)}, f32[512,128]{1,0:T(8,128)S(1)}) custom-call(f32[128,256]{1,0:T(8,128)S(1)} %get-tuple-element.35.refs_0_, s32[1,512]{1,0:T(1,128)S(1)} %get-tuple-element.27.refs_0_.refs_1_, f32[512,256]{1,0:T(8,128)S(1)} %get-tuple-element.36.refs_2_, f32[512,128]{1,0:T(8,128)S(1)} %get-tuple-element.37.refs_3_), custom_call_target="tpu_custom_call" | custom-call | flops 1000000000 | tf_op jit(solution)/shard_map/pallas_call | solution.py:267
  14.7 1.8 %collective-permute-done.3.refs_2_ = f32[128,128]{1,0:T(8,128)S(1)} collective-permute-done((f32[128,128]{1,0:T(8,128)S(1)}, f32[128,128]{1,0:T(8,128)S(1)}, u32[]{:S(2)}, u32[]{:S(2)}) %collective-permute-start.3) | collective-permute-done | bytes 65568 | tf_op jit(solution)/shard_map/ppermute | solution.py:280
  16.5 4.1 %shard_map.69 = (f32[128,128]{1,0:T(8,128)S(1)}, f32[128,128]{1,0:T(8,128)S(1)}, f32[128,128]{1,0:T(8,128)S(1)}) custom-call(f32[512,128]{1,0:T(8,128)S(1)} %get-tuple-element.38.refs_0_.refs_7_, f32[128,128]{1,0:T(8,128)S(1)} %get-tuple-element.39.refs_1_, f32[128,128]{1,0:T(8,128)S(1)} %collective-permute-done.3.refs_2_, ...), custom_call_target="tpu_custom_call" | custom-call | flops 6000000000 | tf_op jit(solution)/shard_map/pallas_call | solution.py:267
  20.6 3.1 %collective-permute-start.5 = (f32[128,128]{1,0:T(8,128)S(1)}, f32[128,128]{1,0:T(8,128)S(1)}, u32[]{:S(2)}, u32[]{:S(2)}) collective-permute-start(f32[128,128]{1,0:T(8,128)S(1)} %get-tuple-element.46.refs_0_), channel_id=1, source_target_pairs={{0,16},{4,20},{8,24},{12,28},{16,0},{20,4},{24,8},{28,12},{1,17},{... | collective-permute-start | bytes 196616 | tf_op jit(solution)/shard_map/ppermute | solution.py:280
  23.7 0.0 collective-permute-done.2.refs_1_
  23.7 0.9 %shard_map.70 = (f32[128,256]{1,0:T(8,128)S(1)}, f32[512,256]{1,0:T(8,128)S(1)}, f32[512,128]{1,0:T(8,128)S(1)}) custom-call(f32[128,256]{1,0:T(8,128)S(1)} %get-tuple-element.35.refs_0_, f32[128,256]{1,0:T(8,128)S(1)} %collective-permute-done.2.refs_1_, f32[128,128]{1,0:T(8,128)S(1)} %get-tuple-element.40.refs_2_, ...), custom_call_target="tpu_custom_call" | custom-call | flops 1000000000 | tf_op jit(solution)/shard_map/pallas_call | solution.py:267
  24.6 0.1 collective-permute-start.4
  24.7 4.0 %collective-permute-done.5.refs_1_ = f32[128,128]{1,0:T(8,128)S(1)} collective-permute-done((f32[128,128]{1,0:T(8,128)S(1)}, f32[128,128]{1,0:T(8,128)S(1)}, u32[]{:S(2)}, u32[]{:S(2)}) %collective-permute-start.5) | collective-permute-done | bytes 65568 | tf_op jit(solution)/shard_map/ppermute | solution.py:280
  28.7 3.8 %shard_map.71.refs_2_ = f32[128,128]{1,0:T(8,128)S(1)} custom-call(f32[128,128]{1,0:T(8,128)S(1)} %get-tuple-element.46.refs_0_, f32[128,128]{1,0:T(8,128)S(1)} %collective-permute-done.5.refs_1_, bf16[1,3,128,128]{3,2,1,0:T(8,128)(2,1)S(1)} %copy-done.1), custom_call_target="tpu_custom_call" | custom-call | flops 6000000000 | tf_op jit(solution)/shard_map/pallas_call | solution.py:267
  32.6 0.0 collective-permute-done.4.refs_1_
  32.6 1.4 %shard_map.72 = f32[512,256]{1,0:T(8,128)} custom-call(f32[128,256]{1,0:T(8,128)S(1)} %get-tuple-element.45.refs_0_, f32[128,256]{1,0:T(8,128)S(1)} %collective-permute-done.4.refs_1_, f32[128,128]{1,0:T(8,128)S(1)} %shard_map.71.refs_2_, f32[512,256]{1,0:T(8,128)S(1)} %get-tuple-element.47.refs_3_, f32[512,128]{1,0:T(8,128)S(1)} %get-tuple-element.48.refs_4_), custom_call_target="tpu_custom_call" | custom-call | flops 1000000000 | tf_op jit(solution)/shard_map/pallas_call | solution.py:267
  (3 shorter events, 0.0 us)
Async XLA Ops:
  0.0 5.0 %copy-start = (f32[512,256]{1,0:T(8,128)S(1)}, f32[512,256]{1,0:T(8,128)}, u32[]{:S(2)}) copy-start(f32[512,256]{1,0:T(8,128)} %refs_1_.3) | copy-start | bytes 1572868
  2.0 5.3 %collective-permute-start.1 = (f32[128,128]{1,0:T(8,128)S(1)}, f32[128,128]{1,0:T(8,128)S(1)}, u32[]{:S(2)}, u32[]{:S(2)}) collective-permute-start(f32[128,128]{1,0:T(8,128)S(1)} %get-tuple-element.32.refs_0_), channel_id=1, source_target_pairs={{0,4},{4,0},{8,12},{12,8},{16,20},{20,16},{24,28},{28,24},{1,5},{5... | collective-permute-start | bytes 196616 | tf_op jit(solution)/shard_map/ppermute | solution.py:280
  5.0 2.2 %copy-start.1 = (bf16[1,3,128,128]{3,2,1,0:T(8,128)(2,1)S(1)}, bf16[1,3,128,128]{3,2,1,0:T(8,128)(2,1)}, u32[]{:S(2)}) copy-start(bf16[1,3,128,128]{3,2,1,0:T(8,128)(2,1)} %refs_2_.5) | copy-start | bytes 294916
  5.0 2.2 %copy-start.2 = (bf16[1,2,128,128]{3,2,1,0:T(8,128)(2,1)S(1)}, bf16[1,2,128,128]{3,2,1,0:T(8,128)(2,1)}, u32[]{:S(2)}) copy-start(bf16[1,2,128,128]{3,2,1,0:T(8,128)(2,1)} %refs_4_.1) | copy-start | bytes 196612
  6.9 6.7 %collective-permute-start = (f32[128,256]{1,0:T(8,128)S(1)}, f32[128,256]{1,0:T(8,128)S(1)}, u32[]{:S(2)}, u32[]{:S(2)}) collective-permute-start(f32[128,256]{1,0:T(8,128)S(1)} %get-tuple-element.31.refs_0_), channel_id=1, source_target_pairs={{0,4},{4,0},{8,12},{12,8},{16,20},{20,16},{24,28},{28,24},{1,5},{5... | collective-permute-start | bytes 393224 | tf_op jit(solution)/shard_map/ppermute | solution.py:280
  11.4 5.0 %collective-permute-start.3 = (f32[128,128]{1,0:T(8,128)S(1)}, f32[128,128]{1,0:T(8,128)S(1)}, u32[]{:S(2)}, u32[]{:S(2)}) collective-permute-start(f32[128,128]{1,0:T(8,128)S(1)} %get-tuple-element.39.refs_1_), channel_id=1, source_target_pairs={{0,8},{4,12},{8,0},{12,4},{16,24},{20,28},{24,16},{28,20},{1,9},{5... | collective-permute-start | bytes 196616 | tf_op jit(solution)/shard_map/ppermute | solution.py:280
  13.8 9.8 %collective-permute-start.2 = (f32[128,256]{1,0:T(8,128)S(1)}, f32[128,256]{1,0:T(8,128)S(1)}, u32[]{:S(2)}, u32[]{:S(2)}) collective-permute-start(f32[128,256]{1,0:T(8,128)S(1)} %get-tuple-element.35.refs_0_), channel_id=1, source_target_pairs={{0,8},{4,12},{8,0},{12,4},{16,24},{20,28},{24,16},{28,20},{1,9},{5... | collective-permute-start | bytes 393224 | tf_op jit(solution)/shard_map/ppermute | solution.py:280
  20.6 8.1 %collective-permute-start.5 = (f32[128,128]{1,0:T(8,128)S(1)}, f32[128,128]{1,0:T(8,128)S(1)}, u32[]{:S(2)}, u32[]{:S(2)}) collective-permute-start(f32[128,128]{1,0:T(8,128)S(1)} %get-tuple-element.46.refs_0_), channel_id=1, source_target_pairs={{0,16},{4,20},{8,24},{12,28},{16,0},{20,4},{24,8},{28,12},{1,17},{... | collective-permute-start | bytes 196616 | tf_op jit(solution)/shard_map/ppermute | solution.py:280
  24.6 8.0 %collective-permute-start.4 = (f32[128,256]{1,0:T(8,128)S(1)}, f32[128,256]{1,0:T(8,128)S(1)}, u32[]{:S(2)}, u32[]{:S(2)}) collective-permute-start(f32[128,256]{1,0:T(8,128)S(1)} %get-tuple-element.45.refs_0_), channel_id=1, source_target_pairs={{0,16},{4,20},{8,24},{12,28},{16,0},{20,4},{24,8},{28,12},{1,17},{... | collective-permute-start | bytes 393224 | tf_op jit(solution)/shard_map/ppermute | solution.py:280
